TPU v7x, 32 devices: a whole 2x2x4 slice. The times are simulated.
32 devices in a mesh: row: 4 (over y, x), sim: 8 (over z, core).
Axes of the slice: x: 2, y: 2, z: 4, core: 2. Of those that a mesh axis runs over, the one named last changes fastest.
Arguments:
- right_side: float32 [6144, 10240], P('row', 'sim'), may hold values from -6 to 6
- lower_panels: float32 [3, 6144, 512], P(None, ('row', 'sim')), may hold values from -0.15625 to 0.15625
- inverse_blocks: float32 [3, 512, 512], replicated, may hold values from -1 to 1.5, as said below
Outputs:
- solved: float32 [1536, 10240], P('row', 'sim')
- updated: float32 [6144, 10240], P('row', 'sim')
Inputs may be any that keep to these rules, and one draw needn't show every extreme that they name: `inverse_blocks`: each block is lower triangular with a diagonal between 0.5 and 1.5.
All inputs are finite; a program needn't handle non-finite values.
Results may differ from a plain program's by a relative error of at most 0.0001.
Values sent between devices are 32-bit elements; how exact they have to be, the bound alone decides.
A program may use at most 128 MiB of HBM per device.

v0:
```python
import jax
import jax.numpy as jnp
from jax import lax
from jax.sharding import PartitionSpec as P

NB = 512
PANELS = 3


def from_root(array, axis, root):
    mine = lax.axis_index(axis) == root
    return lax.psum(jnp.where(mine, array, jnp.zeros_like(array)), axis)


def solve_block(leading, inverse, panel):
    candidate = jnp.dot(
        inverse, leading, precision=lax.Precision.HIGHEST, preferred_element_type=jnp.float32
    )
    return from_root(candidate, "row", panel)


def local(right_side, lower_panels, inverse_blocks):
    row_count = lax.axis_size("row")
    row_index = lax.axis_index("row")
    local_rows = right_side.shape[0]
    row_block = jnp.arange(local_rows) // NB * row_count + row_index
    solved_list = []
    gathered = lax.all_gather(lower_panels, "sim", axis=1, tiled=True)
    leading = right_side[:NB]
    for panel in range(PANELS):
        corrected = leading
        for earlier in range(panel):
            corrected = corrected - jnp.dot(
                gathered[earlier, :NB],
                solved_list[earlier],
                precision=lax.Precision.HIGHEST,
                preferred_element_type=jnp.float32,
            )
        solved_list.append(solve_block(corrected, inverse_blocks[panel], panel))
    stacked = jnp.concatenate(solved_list, 0)
    keeping = (row_block[None, :] > jnp.arange(PANELS)[:, None]).astype(jnp.float32)
    masked = gathered * keeping[:, :, None]
    flat = masked.transpose(1, 0, 2).reshape(local_rows, PANELS * NB)
    right_side = right_side - jnp.dot(
        flat, stacked, precision=lax.Precision.HIGHEST, preferred_element_type=jnp.float32
    )
    share = stacked.shape[0] // row_count
    solved = lax.dynamic_slice_in_dim(stacked, row_index * share, share, 0)
    return (solved, right_side)


def solution(mesh):
    placed = (P("row", "sim"), P(None, ("row", "sim"), None), P())
    return jax.shard_map(
        local,
        mesh=mesh,
        in_specs=placed,
        out_specs=(P("row", "sim"), P("row", "sim")),
        check_vma=False,
    )
```

profile of v0, /device:TPU:3, one launch (start us, length us, event | category | flops | bytes accessed | tf_op | source)
XLA Modules:
  0.0 360.7 jit_solution(10545992417098183838)
XLA Ops:
  8.0 0.0 all-reduce.4.cloned.1.call-start
  8.0 8.0 %convolution_select_fusion.2 = f32[512,1280]{1,0:T(8,128)} fusion(pred[]{:T(512)S(6)} %eq.9, f32[3,512,512]{2,1,0:T(8,128)} %param.5, f32[1536,1280]{1,0:T(8,128)} %param.3), kind=kOutput, calls=%fused_computation.4 | convolution fusion | flops 4027187200 | bytes 6291457 | tf_op jit(solution)/shard_map/dot_general | solution.py:16
  16.0 0.0 all-reduce.4.cloned.1.call-update
  16.0 0.0 all-gather.2.cloned.1.call-start
  16.1 0.5 all-gather.2.cloned.1.call-update
  16.6 0.0 slice-start
  16.6 0.0 all-reduce.6.cloned.1.call-start
  16.7 1.7 slice-done
  18.4 2.3 copy.18
  20.6 75.2 %all-reduce.4.cloned.1.call-done = f32[512,1280]{1,0:T(8,128)} async-done(((f32[512,1280]{1,0:T(8,128)}), f32[512,1280]{1,0:T(8,128)}) %all-reduce.4.cloned.1.call-update) | async-done | bytes 2621456 | tf_op jit(solution)/shard_map/psum | solution.py:12
  95.8 14.6 %all-gather.2.cloned.1.call-done = f32[3,1536,512]{2,1,0:T(8,128)} async-done(((f32[3,192,512]{2,1,0:T(8,128)}), f32[3,1536,512]{2,1,0:T(8,128)}) %all-gather.2.cloned.1.call-update) | async-done | bytes 9437200 | tf_op jit(solution)/shard_map/all_gather | solution.py:28
  110.5 11.2 %fusion.3 = f32[512,1280]{0,1:T(8,128)S(1)} fusion(f32[512,1280]{0,1:T(8,128)} %copy.18, f32[512,1280]{1,0:T(8,128)} %all-reduce.4.cloned.1.call-done, f32[3,1536,512]{2,1,0:T(8,128)} %all-gather.2.cloned.1.call-done), kind=kOutput, calls=%fused_computation.10 | convolution fusion | flops 4027187200 | bytes 8912896 | tf_op jit(solution)/shard_map/dot_general | solution.py:33
  121.6 7.5 %fusion = f32[512,1280]{1,0:T(8,128)} fusion(f32[512,1280]{0,1:T(8,128)S(1)} %fusion.3, pred[]{:T(512)S(6)} %eq.10, f32[3,512,512]{2,1,0:T(8,128)} %param.5), kind=kOutput, calls=%fused_computation.5 | convolution fusion | flops 4027187200 | bytes 6291457 | tf_op jit(solution)/shard_map/dot_general | solution.py:16
  129.1 0.0 all-reduce.6.cloned.1.call-update
  129.2 0.0 all-reduce.8.cloned.1.call-start
  129.2 76.5 %all-reduce.6.cloned.1.call-done = f32[512,1280]{1,0:T(8,128)} async-done(((f32[512,1280]{1,0:T(8,128)}), f32[512,1280]{1,0:T(8,128)}) %all-reduce.6.cloned.1.call-update) | async-done | bytes 2621456 | tf_op jit(solution)/shard_map/psum | solution.py:12
  205.7 10.5 %fusion.2 = f32[512,1280]{0,1:T(8,128)S(1)} fusion(f32[512,1280]{0,1:T(8,128)S(1)} %fusion.3, f32[512,1280]{1,0:T(8,128)} %all-reduce.6.cloned.1.call-done, f32[3,1536,512]{2,1,0:T(8,128)} %all-gather.2.cloned.1.call-done), kind=kOutput, calls=%fused_computation.8 | convolution fusion | flops 4027187200 | bytes 8912896 | tf_op jit(solution)/shard_map/dot_general | solution.py:33
  216.3 7.3 %fusion.1 = f32[512,1280]{1,0:T(8,128)} fusion(f32[512,1280]{0,1:T(8,128)S(1)} %fusion.2, pred[]{:T(512)S(6)} %eq.11, f32[3,512,512]{2,1,0:T(8,128)} %param.5), kind=kOutput, calls=%fused_computation.6 | convolution fusion | flops 4027187200 | bytes 6291457 | tf_op jit(solution)/shard_map/dot_general | solution.py:16
  223.5 0.0 copy-start
  223.5 0.0 all-reduce.8.cloned.1.call-update
  223.6 1.7 copy-done
  225.3 1.7 constant_dynamic-update-slice_fusion.2
  226.9 9.7 %copy.15 = f32[3,1536,512]{1,2,0:T(8,128)} copy(f32[3,1536,512]{2,1,0:T(8,128)} %all-gather.2.cloned.1.call-done) | data formatting | bytes 18874368 | tf_op jit(solution)/shard_map/all_gather | solution.py:28
  236.7 0.0 copy-start.1
  236.7 9.1 %broadcast_multiply_fusion = f32[3,1536,512]{1,2,0:T(8,128)} fusion(f32[3,1536,512]{1,2,0:T(8,128)} %copy.15, f32[3,1536]{1,0:T(4,128)S(1)} %fusion.10), kind=kLoop, calls=%fused_computation.1 | loop fusion | flops 2359296 | bytes 18892800 | tf_op jit(solution)/shard_map/mul | solution.py:42
  245.7 0.0 copy-done.1
  245.7 1.7 constant_dynamic-update-slice_fusion.1
  247.4 54.7 %all-reduce.8.cloned.1.call-done = f32[512,1280]{1,0:T(8,128)} async-done(((f32[512,1280]{1,0:T(8,128)}), f32[512,1280]{1,0:T(8,128)}) %all-reduce.8.cloned.1.call-update) | async-done | bytes 2621456 | tf_op jit(solution)/shard_map/psum | solution.py:12
  302.1 3.5 constant_dynamic-update-slice_fusion
  305.6 44.8 %convolution_subtract_fusion = f32[1536,1280]{1,0:T(8,128)} fusion(f32[1536,1280]{1,0:T(8,128)} %param.3, f32[1536,1536]{0,1:T(8,128)} %bitcast.36, f32[1536,1280]{1,0:T(8,128)} %constant_dynamic-update-slice_fusion), kind=kOutput, calls=%fused_computation | convolution fusion | flops 36240752640 | bytes 33030144 | tf_op jit(solution)/shard_map/dot_general | solution.py:44
  350.4 2.9 constant_dynamic-slice_fusion
  (2 shorter events, 0.0 us)
Async XLA Ops:
  8.0 87.8 %all-reduce.4.cloned.1.call-start = ((), (), s32[]{:S(2)}) async-start(), calls=%async_computation | async-start | bytes 5242880 | tf_op jit(solution)/shard_map/psum | solution.py:12
  16.0 94.5 %all-gather.2.cloned.1.call-start = ((), (), s32[]{:S(2)}) async-start(), calls=%async_computation.1 | async-start | bytes 10616832 | tf_op jit(solution)/shard_map/all_gather | solution.py:28
  16.6 1.7 slice-start
  16.6 189.1 %all-reduce.6.cloned.1.call-start = ((), (), s32[]{:S(2)}) async-start(), calls=%async_computation.2 | async-start | bytes 5242880 | tf_op jit(solution)/shard_map/psum | solution.py:12
  129.2 173.0 %all-reduce.8.cloned.1.call-start = ((), (), s32[]{:S(2)}) async-start(), calls=%async_computation.3 | async-start | bytes 5242880 | tf_op jit(solution)/shard_map/psum | solution.py:12
  223.5 1.7 copy-start
  236.7 9.1 %copy-start.1 = (f32[512,1280]{1,0:T(8,128)S(1)}, f32[512,1280]{1,0:T(8,128)}, u32[]{:S(2)}) copy-start(f32[512,1280]{1,0:T(8,128)} %all-reduce.6.cloned.1.call-done) | copy-start | bytes 7864324
Sparse Core Ops, SparseCore 0:
  16.1 79.6 all-reduce.3
  129.3 76.4 all-reduce.5
  223.7 78.4 all-reduce.7
Sparse Core Ops, SparseCore 1:
  18.2 92.2 all-gather.1
where the time goes:
time: 366 us; the launch traced here: 361 us
  waiting for transfers between devices  222 us (61%)
  matrix products  89.2 us (24%)
  local copies, waits for them, and re-layouts  25.1 us (7%)
  between operations  15.4 us (4%)
  other arithmetic  9.09 us (2%)
    psum x3, waiting for transfers between devices, from_root(): return lax.psum(jnp.where(mine, array, jnp.zeros_like(array)), axis)  206 us
    dot_general x1, matrix products, local(): jnp.dot(flat, stacked, precision=lax.Precision.HIGHEST, preferred_element...  44.8 us
    dot_general x3, matrix products, solve_block(): jnp.dot(inverse, leading, precision=lax.Precision.HIGHEST, preferred_elem...  22.7 us
    dot_general x2, matrix products, local(): jnp.dot(gathered[earlier, :NB], solved_list[earlier], precision=lax.Preci...  21.7 us
    all_gather x1, waiting for transfers between devices, local(): gathered = lax.all_gather(lower_panels, 'sim', axis=1, tiled=True)  14.6 us
    all_gather x1, local copies, waits for them, and re-layouts, local(): gathered = lax.all_gather(lower_panels, 'sim', axis=1, tiled=True)  9.73 us
    mul x1, other arithmetic, local(): masked = gathered * keeping[:, :, None]  9.07 us
    unnamed x9, local copies, waits for them, and re-layouts  8.97 us
  transfers between devices with their start and end apart: 4, of which 4 were waited for; matrix products, arithmetic and copies ran while one was open for 7% of the time, Pallas kernels for 0%

commit v1 on v0

v1 whole, which is shorter than its diff:
```python
import functools
import math

import jax
import jax.numpy as jnp
from jax import lax
from jax.experimental import pallas as pl
from jax.experimental.pallas import tpu as pltpu
from jax.sharding import PartitionSpec as P

MESH = pl.DeviceIdType.MESH
CHUNK = 256
TILE = 256


def split(x):
    high = x.astype(jnp.bfloat16)
    return high, (x - high.astype(jnp.float32)).astype(jnp.bfloat16)


def mul(a, b):
    return jnp.dot(a, b, preferred_element_type=jnp.float32)


def ring_position(row, rows):
    return row // 2 if row % 2 == 0 else rows - 1 - row // 2


def kernel(R, S, b_hbm, l_hbm, inv_hbm, solved_hbm, upd_hbm, bv, lg, lh, ll, yv, yh, yl, iv, ih, il,
           lrecv, lsend, lown, yrecv, ysend, bsem, isem, osem, ssem):
    panels, chunks, nb, width = yv.shape
    rows = bv.shape[1]
    h = lg.shape[2]
    Z = S // 2
    r, s = lax.axis_index("row"), lax.axis_index("sim")
    z, core = s // 2, s % 2
    partner = s + 1 - 2 * core
    half = R // 2
    pos = jnp.where(r % 2 == 0, r // 2, R - 1 - r // 2)

    def row_at(position):
        q = lax.rem(position + R, R)
        return jnp.where(q < half, 2 * q, 2 * (R - 1 - q) + 1)

    right, left = row_at(pos + 1), row_at(pos - 1)
    up, down = lax.rem(s + 2, S), lax.rem(s + S - 2, S)

    barrier = pltpu.get_barrier_semaphore()
    for target in ((right, s), (left, s), (r, up), (r, down), (r, partner)):
        pl.semaphore_signal(barrier, inc=1, device_id=target, device_id_type=MESH)

    own_copies = [pltpu.make_async_copy(l_hbm.at[p], lg.at[p, s], lown.at[p]) for p in range(panels)]
    solver = r < panels
    inv_copy = pltpu.make_async_copy(inv_hbm.at[jnp.minimum(r, panels - 1)], iv, isem)
    inv_copy.start()
    b_copies = [
        pltpu.make_async_copy(b_hbm.at[:, pl.ds(c * width, width)], bv.at[c], bsem.at[c]) for c in range(chunks)
    ]
    b_copies[0].start()
    for copy in own_copies:
        copy.start()
    for copy in b_copies[1:]:
        copy.start()
    pl.semaphore_wait(barrier, 5)

    pending = []

    def send(cond, make):
        @pl.when(cond)
        def _():
            make().start()

        pending.append((cond, make))

    def l_copy(p, slot, way, target, own):
        src = l_hbm.at[p] if own else lg.at[p, slot]
        return pltpu.make_async_remote_copy(
            src_ref=src, dst_ref=lg.at[p, slot], send_sem=lsend.at[way, p, slot], recv_sem=lrecv.at[p, slot],
            device_id=(r, target), device_id_type=MESH,
        )

    def l_up(p, zz):
        slot = 2 * zz + core
        send(z == zz, lambda: l_copy(p, slot, 0, up, True))

        @pl.when(z > zz)
        def _():
            l_copy(p, slot, 0, up, False).wait_recv()

        send((z > zz) & (z < Z - 1), lambda: l_copy(p, slot, 0, up, False))
        send(z > zz, lambda: l_copy(p, slot, 2, partner, False))

    def l_down(p, zz):
        slot = 2 * zz + core
        send(z == zz, lambda: l_copy(p, slot, 1, down, True))

        @pl.when(z < zz)
        def _():
            l_copy(p, slot, 1, down, False).wait_recv()

        send((z < zz) & (z > 0), lambda: l_copy(p, slot, 1, down, False))
        send(z < zz, lambda: l_copy(p, slot, 2, partner, False))

    own_waited = set()

    def convert(p, zz):
        if p not in own_waited:
            own_waited.add(p)
            own_copies[p].wait()
        l_copy(p, 2 * zz + 1 - core, 2, partner, False).wait_recv()
        for k in range(2):
            first = (2 * zz + k) * h
            value = lg[p, 2 * zz + k]
            if first // nb * R <= p:
                row = first + lax.broadcasted_iota(jnp.int32, (h, 1), 0)
                block = jnp.where(row < nb * (first // nb + 1), first // nb, first // nb + 1) * R + r
                value = jnp.where(block > p, value, 0.0)
            high, low = split(value)
            lh[p, first:first + h] = high
            ll[p, first:first + h] = low

    lead = min(Z, -(-nb // (2 * h)))
    ups = [(panels - 1, zz) for zz in range(lead, Z - 1)]
    ups += [(p, zz) for p in range(panels - 1) for zz in range(min(lead, Z - 1))]
    ups += [(p, zz) for p in range(panels) for zz in reversed(range(Z - 1)) if (p, zz) not in ups]
    downs = [(p, zz) for p in range(panels - 1) for zz in range(1, lead)]
    downs += [(p, zz) for p in range(panels) for zz in range(1, Z) if (p, zz) not in downs]
    state = {"next": 0}
    seen_up, seen_down, converted = set(), set(), set()

    def l_step():
        i = state["next"]
        if i >= len(ups):
            return
        state["next"] += 1
        l_up(*ups[i])
        l_down(*downs[i])
        seen_up.add(ups[i])
        seen_down.add(downs[i])

    def l_convert():
        for p in range(panels):
            for zz in range(Z):
                ready = ((p, zz) in seen_up or zz == Z - 1) and ((p, zz) in seen_down or zz == 0)
                if ready and (p, zz) not in converted:
                    converted.add((p, zz))
                    convert(p, zz)

    def l_need(p, count):
        while not all(((p, zz) in seen_up or zz == Z - 1) and ((p, zz) in seen_down or zz == 0) for zz in range(count)):
            l_step()
        l_convert()

    def y_copy(k, c, way, target):
        return pltpu.make_async_remote_copy(
            src_ref=yv.at[k, c], dst_ref=yv.at[k, c], send_sem=ysend.at[way, k, c], recv_sem=yrecv.at[k, c],
            device_id=(target, s), device_id_type=MESH,
        )

    def reach(k, c):
        if k == 0:
            rightward = half if 5 * c < 3 * chunks else half - 1
        else:
            rightward = half - 1 if k == 1 else half
        return rightward, R - 1 - rightward

    def distance(k):
        return lax.rem(pos - ring_position(k, R) + R, R)

    def y_make(k, c):
        @pl.when(r == k)
        def _():
            high, low = split(bv[c, 0:nb])

            def body(i, carry):
                rows_i = pl.ds(pl.multiple_of(i * TILE, TILE), TILE)
                value = mul(ih[rows_i], high) + mul(ih[rows_i], low) + mul(il[rows_i], high)
                yv[k, c, rows_i] = value
                top, rest = split(value)
                yh[k, c, rows_i] = top
                yl[k, c, rows_i] = rest
                return carry

            lax.fori_loop(0, nb // TILE, body, 0)

        send(r == k, lambda: y_copy(k, c, 0, right))
        if reach(k, c)[1] > 0:
            send(r == k, lambda: y_copy(k, c, 1, left))

    def y_recv(k, c):
        @pl.when(r != k)
        def _():
            y_copy(k, c, 0, right).wait_recv()

        d = distance(k)
        rightward, leftward = reach(k, c)
        if rightward > 1:
            send((d > 0) & (d < rightward), lambda: y_copy(k, c, 0, right))
        if leftward > 1:
            send((d > 0) & (R - d < leftward), lambda: y_copy(k, c, 1, left))

        @pl.when(r != k)
        def _():
            top, rest = split(yv[k, c])
            yh[k, c] = top
            yl[k, c] = rest

    def update(ps, c, start, count):
        def body(i, carry):
            rows_i = pl.ds(pl.multiple_of(start + i * TILE, TILE), TILE)
            total = None
            for p in ps:
                part = mul(lh[p, rows_i], yh[p, c]) + mul(lh[p, rows_i], yl[p, c]) + mul(ll[p, rows_i], yh[p, c])
                total = part if total is None else total + part
            bv[c, rows_i] = bv[c, rows_i] - total
            return carry

        lax.fori_loop(0, count // TILE, body, 0)

    def y_lead(k, c):
        @pl.when(r > k)
        def _():
            update((k,), c, 0, nb)

    def rest(ps, c):
        update(ps, c, nb, rows - nb)

    outs = []

    def write(c):
        copy = pltpu.make_async_copy(bv.at[c], upd_hbm.at[:, pl.ds(c * width, width)], osem.at[c])
        copy.start()
        outs.append(copy)
        share = solved_hbm.shape[0]
        piece = math.gcd(share, nb)
        for i in range(share // piece):
            q = r * share + i * piece
            source = yv.at[q // nb, c, pl.ds(pl.multiple_of(q % nb, piece), piece)]
            copy = pltpu.make_async_copy(
                source, solved_hbm.at[pl.ds(i * piece, piece), pl.ds(c * width, width)], ssem.at[i, c]
            )
            copy.start()
            outs.append(copy)

    for p in range(panels):
        send(z >= 0, lambda p=p: l_copy(p, s, 2, partner, True))
    l_step()
    inv_copy.wait()

    @pl.when(solver)
    def _():
        high, low = split(iv[...])
        ih[...] = high
        il[...] = low

    for c in range(chunks):
        b_copies[c].wait()
        y_make(0, c)

    lags = [0] * panels
    for k in range(1, panels):
        lags[k] = 2 * k
    steps = chunks + 2 * (panels - 1)
    per_step = -(-len(ups) // steps)
    early, late = set(), set()
    for t in range(steps):
        for _ in range(per_step):
            l_step()
        for k in range(panels):
            c = t - 2 * k
            if 0 <= c < chunks:
                y_recv(k, c)
            if k + 1 < panels:
                c -= 1
                todo = [c] if 0 <= c < chunks else []
                for c in todo:
                    l_need(k, lead)
                    y_lead(k, c)
                    y_make(k + 1, c)
        if len(seen_up) == len(ups) or t >= steps - 3:
            l_convert()
        ready = [p for p in range(panels - 1) if all((p, zz) in converted for zz in range(Z))]
        if len(ready) == panels - 1:
            budget = 0
            for c in range(chunks):
                if c <= t - 2 * (panels - 2) and c not in early and budget < 2:
                    early.add(c)
                    budget += 1
                    rest(tuple(ready), c)
    while state["next"] < len(ups):
        l_step()
    l_convert()
    for c in range(chunks):
        if c not in early:
            rest(tuple(range(panels - 1)), c)
        y_lead(panels - 1, c)
        rest((panels - 1,), c)
        write(c)
    for copy in outs:
        copy.wait()
    for cond, make in pending:
        @pl.when(cond)
        def _(make=make):
            make().wait_send()


def local(R, S, right_side, lower_panels, inverse_blocks):
    rows, columns = right_side.shape
    panels, h, nb = lower_panels.shape
    chunks = columns // CHUNK
    share = panels * nb // R
    f32, bf16 = jnp.float32, jnp.bfloat16
    dma = pltpu.SemaphoreType.DMA
    anywhere = pl.BlockSpec(memory_space=pl.ANY)
    return pl.pallas_call(
        functools.partial(kernel, R, S),
        out_shape=(jax.ShapeDtypeStruct((share, columns), f32), jax.ShapeDtypeStruct((rows, columns), f32)),
        in_specs=[anywhere] * 3,
        out_specs=(anywhere, anywhere),
        scratch_shapes=[
            pltpu.VMEM((chunks, rows, CHUNK), f32),
            pltpu.VMEM((panels, S, h, nb), f32),
            pltpu.VMEM((panels, rows, nb), bf16),
            pltpu.VMEM((panels, rows, nb), bf16),
            pltpu.VMEM((panels, chunks, nb, CHUNK), f32),
            pltpu.VMEM((panels, chunks, nb, CHUNK), bf16),
            pltpu.VMEM((panels, chunks, nb, CHUNK), bf16),
            pltpu.VMEM((nb, nb), f32),
            pltpu.VMEM((nb, nb), bf16),
            pltpu.VMEM((nb, nb), bf16),
            dma((panels, S)),
            dma((3, panels, S)),
            dma((panels,)),
            dma((panels, chunks)),
            dma((2, panels, chunks)),
            dma((chunks,)),
            dma,
            dma((chunks,)),
            dma((share // math.gcd(share, nb), chunks)),
        ],
        compiler_params=pltpu.CompilerParams(
            collective_id=0, has_side_effects=True, vmem_limit_bytes=58 * 1024 * 1024
        ),
        cost_estimate=pl.CostEstimate(
            flops=6 * rows * panels * nb * columns, bytes_accessed=8 * rows * columns, transcendentals=0
        ),
    )(right_side, lower_panels, inverse_blocks)


def solution(mesh):
    placed = (P("row", "sim"), P(None, ("row", "sim"), None), P())
    return jax.shard_map(
        functools.partial(local, mesh.shape["row"], mesh.shape["sim"]),
        mesh=mesh,
        in_specs=placed,
        out_specs=(P("row", "sim"), P("row", "sim")),
        check_vma=False,
    )
```

time: 366 us -> 318 us (0.87); the launches traced: 361 us -> 318 us
  Pallas kernels: 0 us -> 308 us
  waiting for transfers between devices: 222 us -> 0 us
  matrix products: 89.2 us -> 0 us
  local copies, waits for them, and re-layouts: 25.1 us -> 9.9 us
  between operations: 15.4 us -> 0.64 us
  other arithmetic: 9.09 us -> 0 us
    pallas_call x0 -> x1, Pallas kernels: none -> 308 us  [local(): pl.pallas_call(functools.partial(kernel, R, S), out_shape=(jax.ShapeDtype...]
    psum x3 -> x0, waiting for transfers between devices: 206 us -> none  [from_root(): return lax.psum(jnp.where(mine, array, jnp.zeros_like(array)), axis)]
    dot_general x6 -> x0, matrix products: 89.2 us -> none  [the longest x1 44.8 us: local(): jnp.dot(flat, stacked, precision=lax.Precision.HIGHEST, preferred_element...]
    all_gather x1 -> x0, waiting for transfers between devices: 14.6 us -> none  [local(): gathered = lax.all_gather(lower_panels, 'sim', axis=1, tiled=True)]
    all_gather x1 -> x0, local copies, waits for them, and re-layouts: 9.73 us -> none  [local(): gathered = lax.all_gather(lower_panels, 'sim', axis=1, tiled=True)]
    mul x1 -> x0, other arithmetic: 9.07 us -> none  [local(): masked = gathered * keeping[:, :, None]]
    unnamed x9 -> x2, local copies, waits for them, and re-layouts: 8.97 us -> 9.9 us
  transfers between devices with their start and end apart: 4 -> 0, of which waited for: 4 -> 0; matrix products, arithmetic and copies ran while one was open for 7% -> 0% of each run, Pallas kernels for 0% -> 0%
where the time goes in v1:
time: 318 us
  Pallas kernels  308 us (97%)
  local copies, waits for them, and re-layouts  9.9 us (3%)
    pallas_call x1, Pallas kernels, local(): pl.pallas_call(functools.partial(kernel, R, S), out_shape=(jax.ShapeDtype...  308 us
    unnamed x2, local copies, waits for them, and re-layouts  9.9 us

profile of v1, /device:TPU:3, one launch (start us, length us, event | category | flops | bytes accessed | tf_op | source)
XLA Modules:
  0.0 318.1 jit_solution(2400702550065231298)
XLA Ops:
  0.6 307.6 %shard_map.50 = (f32[384,1280]{1,0:T(8,128)}, f32[1536,1280]{1,0:T(8,128)}) custom-call(f32[1536,1280]{1,0:T(8,128)} %b_hbm.1, f32[3,192,512]{2,1,0:T(8,128)} %l_hbm.1, f32[3,512,512]{2,1,0:T(8,128)} %inv_hbm.1), custom_call_target="tpu_custom_call" | custom-call | flops 18119393280 | bytes 15728640 | tf_op jit(solution)/shard_map/pallas_call | solution.py:315
  308.2 2.9 copy.7
  311.2 7.0 %copy.8 = f32[1536,1280]{1,0:T(8,128)} copy(f32[1536,1280]{1,0:T(8,128)} %get-tuple-element.5) | data formatting | bytes 15728640

commit v2 on v1

v2 whole, which is shorter than its diff:
```python
import functools
import heapq
import itertools
import math

import jax
import jax.numpy as jnp
from jax import lax
from jax.experimental import pallas as pl
from jax.experimental.pallas import tpu as pltpu
from jax.sharding import PartitionSpec as P

MESH = pl.DeviceIdType.MESH
CHUNK = 256
TILE = 256
PARTS = 2
HOP = 1.0
STEP = 1.5
L_TIME = 3.93
Y_TIME = 5.25


def split(x):
    high = x.astype(jnp.bfloat16)
    return high, (x - high.astype(jnp.float32)).astype(jnp.bfloat16)


def mul(a, b):
    return jnp.dot(a, b, preferred_element_type=jnp.float32)


def ring_position(row, rows):
    return row // 2 if row % 2 == 0 else rows - 1 - row // 2


def line_plan(Z, panels, halves, lead, nb, h, upward):
    free, pending = [0.0] * Z, [[] for _ in range(Z)]

    def rank(piece):
        p, zz, j = piece
        source = zz if upward else Z - 1 - zz
        first = p < panels - 1 and source < lead
        return (0, p, zz, j) if first else (1, p, -zz, j)

    for zz in range(Z - 1):
        pending[zz] = [(0.0, (p, zz, j)) for p in range(panels) for j in range(halves)]
    sends, arrivals = [], {}
    while any(pending):
        start, link = min((max(free[q], min(t for t, _ in pending[q])), q) for q in range(Z) if pending[q])
        ready = [entry for entry in pending[link] if entry[0] <= start]
        entry = min(ready, key=lambda e: rank(e[1]))
        pending[link].remove(entry)
        piece = entry[1]
        free[link] = start + L_TIME
        arrival = start + L_TIME + HOP
        real = (lambda q: q) if upward else (lambda q: Z - 1 - q)
        name = (piece[0], real(piece[1]), piece[2])
        sends.append((start if piece[1] == link else entry[0], real(link), name))
        arrivals[name, real(link + 1)] = arrival
        if link + 1 < Z - 1:
            pending[link + 1].append((arrival, piece))
    return sends, arrivals


def ring_sim(R, panels, chunks, parts, lead_ready, reach):
    makes,leads,arr,got,sends={}, {}, {}, {}, []
    busy=[0.0]*panels
    links={}
    heap=[]; n=itertools.count()
    for c in range(chunks):
        makes[0,c]=0.5*c
        for g in range(parts): heapq.heappush(heap,(1+0.5*c+0.1*g,next(n),0,c,g,ring_position(0,R),0,0))
    nextc=[0]*panels
    free={}
    while heap:
        t,_,k,c,g,q,way,left=heapq.heappop(heap)
        if way:
            arr[k,c,g,q]=t
            if all((k,c,x,q) in arr for x in range(parts)): got[k,c,q]=t
        todo=[(way,left)] if way else [(1,reach(k,c,g)),(-1,R-1-reach(k,c,g))]
        for w,l in todo:
            if l>0:
                s=max(t,free.get((q,w),0)); free[q,w]=s+Y_TIME
                heapq.heappush(heap,(s+Y_TIME+HOP,next(n),k,c,g,(q+w)%R,w,l-1))
        for o in range(1,panels):
            p=ring_position(o,R)
            while nextc[o]<chunks and all((e,nextc[o],p) in got for e in range(o)):
                cc=nextc[o]; nextc[o]+=1
                done=busy[o]
                for e in range(o):
                    leads[o,e,cc]=max(done,got[e,cc,p]+0.2,lead_ready[e]); done=leads[o,e,cc]+STEP
                makes[o,cc]=done; busy[o]=done+STEP
                for g2 in range(parts): heapq.heappush(heap,(done+STEP*(g2+1)/parts,next(n),o,cc,g2,p,0,0))
    return arr,got,leads,makes
def kernel(R, S, b_hbm, l_hbm, inv_hbm, solved_hbm, upd_hbm, bv, lg, lh, ll, yv, yh, yl, iv, ih, il,
           lrecv, lsend, lown, yrecv, ysend, bsem, isem, osem, ssem):
    panels, chunks, nb, width = yv.shape
    rows = bv.shape[1]
    h = lg.shape[2]
    Z = S // 2
    sub, seg = h // PARTS, nb // PARTS
    r, s = lax.axis_index("row"), lax.axis_index("sim")
    z, core = s // 2, s % 2
    partner = s + 1 - 2 * core
    half = R // 2
    pos = jnp.where(r % 2 == 0, r // 2, R - 1 - r // 2)

    def row_at(position):
        q = lax.rem(position + R, R)
        return jnp.where(q < half, 2 * q, 2 * (R - 1 - q) + 1)

    right, left = row_at(pos + 1), row_at(pos - 1)
    up, down = lax.rem(s + 2, S), lax.rem(s + S - 2, S)

    barrier = pltpu.get_barrier_semaphore()
    for target in ((right, s), (left, s), (r, up), (r, down), (r, partner)):
        pl.semaphore_signal(barrier, inc=1, device_id=target, device_id_type=MESH)

    own_copies = [pltpu.make_async_copy(l_hbm.at[p], lg.at[p, s], lown.at[p]) for p in range(panels)]
    solver = r < panels
    inv_copy = pltpu.make_async_copy(inv_hbm.at[jnp.minimum(r, panels - 1)], iv, isem)
    inv_copy.start()
    b_copies = [
        pltpu.make_async_copy(b_hbm.at[:, pl.ds(c * width, width)], bv.at[c], bsem.at[c]) for c in range(chunks)
    ]
    b_copies[0].start()
    for copy in own_copies:
        copy.start()
    for copy in b_copies[1:]:
        copy.start()
    pl.semaphore_wait(barrier, 5)

    pending = []

    def send(cond, make):
        @pl.when(cond)
        def _():
            make().start()

        pending.append((cond, make))

    def l_copy(p, slot, j, way, target, own):
        src = l_hbm.at[p, pl.ds(j * sub, sub)] if own else lg.at[p, slot, pl.ds(j * sub, sub)]
        return pltpu.make_async_remote_copy(
            src_ref=src, dst_ref=lg.at[p, slot, pl.ds(j * sub, sub)], send_sem=lsend.at[way, p, slot, j],
            recv_sem=lrecv.at[p, slot, j], device_id=(r, target), device_id_type=MESH,
        )

    def l_send(zz, way, piece):
        p, source, j = piece
        slot, target = 2 * source + core, up if way == 0 else down
        send(z == zz, lambda: l_copy(p, slot, j, way, target, source == zz))

    def l_arrive(zz, piece):
        p, source, j = piece
        slot = 2 * source + core

        @pl.when(z == zz)
        def _():
            l_copy(p, slot, j, 0, up, False).wait_recv()

        send(z == zz, lambda: l_copy(p, slot, j, 2, partner, False))

    own_waited = set()

    def convert(p, zz):
        if p not in own_waited:
            own_waited.add(p)
            own_copies[p].wait()
        for j in range(PARTS):
            l_copy(p, 2 * zz + 1 - core, j, 2, partner, False).wait_recv()
        for k in range(2):
            first = (2 * zz + k) * h
            high, low = split(lg[p, 2 * zz + k])
            lh[p, first:first + h] = high
            ll[p, first:first + h] = low

    def y_copy(k, c, g, way, target):
        part = yv.at[k, c, pl.ds(g * seg, seg)]
        return pltpu.make_async_remote_copy(
            src_ref=part, dst_ref=part, send_sem=ysend.at[way, k, c, g], recv_sem=yrecv.at[k, c, g],
            device_id=(target, s), device_id_type=MESH,
        )

    def reach(k, c, g):
        index, total = c * PARTS + g, chunks * PARTS
        if k == 1:
            return R - 1 if 10 * index < 3 * total else half - 1
        return 0 if 10 * index < (4 if k == 0 else 6) * total else half

    def y_make(k, c):
        @pl.when(r == k)
        def _():
            high, low = split(bv[c, 0:nb])
            for g in range(PARTS):
                part = slice(g * seg, (g + 1) * seg)
                value = mul(ih[part], high) + mul(ih[part], low) + mul(il[part], high)
                yv[k, c, part] = value
                if reach(k, c, g) > 0:
                    y_copy(k, c, g, 0, right).start()
                if reach(k, c, g) < R - 1:
                    y_copy(k, c, g, 1, left).start()
                yh[k, c, part], yl[k, c, part] = split(value)

        for g in range(PARTS):
            if reach(k, c, g) > 0:
                pending.append((r == k, lambda g=g: y_copy(k, c, g, 0, right)))
            if reach(k, c, g) < R - 1:
                pending.append((r == k, lambda g=g: y_copy(k, c, g, 1, left)))

    def y_arrive(k, c, g, q):
        d = (q - ring_position(k, R)) % R
        rightward = reach(k, c, g)
        way = None
        if d < rightward:
            way = 0
        elif d > rightward and R - d < R - 1 - rightward:
            way = 1

        @pl.when(pos == q)
        def _():
            y_copy(k, c, g, 0, right).wait_recv()
            if way is not None:
                y_copy(k, c, g, way, (right, left)[way]).start()

        if way is not None:
            pending.append((pos == q, lambda: y_copy(k, c, g, way, (right, left)[way])))

    def y_split(k, c):
        @pl.when(r != k)
        def _():
            yh[k, c], yl[k, c] = split(yv[k, c])

    def update(ps, c, start, count):
        def body(i, carry):
            rows_i = pl.ds(pl.multiple_of(start + i * TILE, TILE), TILE)
            total = None
            for p in ps:
                part = mul(lh[p, rows_i], yh[p, c]) + mul(lh[p, rows_i], yl[p, c]) + mul(ll[p, rows_i], yh[p, c])
                total = part if total is None else total + part
            bv[c, rows_i] = bv[c, rows_i] - total
            return carry

        lax.fori_loop(0, count // TILE, body, 0)

    def y_lead(o, k, c):
        @pl.when(r == o)
        def _():
            yh[k, c], yl[k, c] = split(yv[k, c])
            update((k,), c, 0, nb)

    def rest(p, c):
        start = jnp.where(solver, nb, 0)
        update((p,), c, start, rows - start)

    outs = []

    def write(c):
        copy = pltpu.make_async_copy(bv.at[c], upd_hbm.at[:, pl.ds(c * width, width)], osem.at[c])
        copy.start()
        outs.append(copy)
        share = solved_hbm.shape[0]
        piece = math.gcd(share, nb)
        for i in range(share // piece):
            q = r * share + i * piece
            source = yv.at[q // nb, c, pl.ds(pl.multiple_of(q % nb, piece), piece)]
            copy = pltpu.make_async_copy(
                source, solved_hbm.at[pl.ds(i * piece, piece), pl.ds(c * width, width)], ssem.at[i, c]
            )
            copy.start()
            outs.append(copy)

    events = []

    def at(time, action, *args):
        events.append((time, len(events), action, args))

    lead = min(Z, -(-nb // (2 * h)))
    converted = {(p, zz): 1.5 for p in range(panels) for zz in range(Z)}
    for way in (0, 1):
        sends, arrivals = line_plan(Z, panels, PARTS, lead, nb, h, way == 0)
        for time, zz, piece in sends:
            own = piece[1] == zz
            at(max(time - 1.5 * L_TIME, -1.0 + 0.001 * time) if own else time + 0.2, l_send, zz, way, piece)
        for (piece, zz), time in arrivals.items():
            at(time + 0.1, l_arrive, zz, piece)
            converted[piece[:2]] = max(converted[piece[:2]], time + 1.5)
    for (p, zz), time in converted.items():
        at(time, convert, p, zz)
    ready = [max(converted[p, zz] for zz in range(lead)) + 0.1 for p in range(panels)]
    whole = [max(converted[p, zz] for zz in range(Z)) + 0.1 for p in range(panels)]
    arrivals, got, leads, makes = ring_sim(R, panels, chunks, PARTS, ready, reach)
    for (k, c), time in makes.items():
        at(time, y_make, k, c)
    for (k, c, g, q), time in arrivals.items():
        at(time, y_arrive, k, c, g, q)
    for (o, k, c), time in leads.items():
        at(time, y_lead, o, k, c)
    for c in range(chunks):
        last = 0.0
        for k in range(panels):
            present = max(time for (a, b, _), time in got.items() if (a, b) == (k, c)) + 0.3
            at(present, y_split, k, c)
            last = max(last, present + 0.1, whole[k] + 0.01 * c)
            at(max(present + 0.1, whole[k] + 0.01 * c), rest, k, c)
        at(last + 0.05, write, c)

    for p in range(panels):
        for j in range(PARTS):
            send(z >= 0, lambda p=p, j=j: l_copy(p, s, j, 2, partner, True))
    events.sort(key=lambda e: e[:2])
    for time, _, action, args in events:
        if time < 0.0:
            action(*args)
    inv_copy.wait()

    @pl.when(solver)
    def _():
        ih[...], il[...] = split(iv[...])

    for copy in b_copies:
        copy.wait()
    for time, _, action, args in events:
        if time >= 0.0:
            action(*args)
    for copy in outs:
        copy.wait()
    for cond, make in pending:
        @pl.when(cond)
        def _(make=make):
            make().wait_send()


def local(R, S, right_side, lower_panels, inverse_blocks):
    rows, columns = right_side.shape
    panels, h, nb = lower_panels.shape
    chunks = columns // CHUNK
    share = panels * nb // R
    f32, bf16 = jnp.float32, jnp.bfloat16
    dma = pltpu.SemaphoreType.DMA
    anywhere = pl.BlockSpec(memory_space=pl.ANY)
    return pl.pallas_call(
        functools.partial(kernel, R, S),
        out_shape=(jax.ShapeDtypeStruct((share, columns), f32), jax.ShapeDtypeStruct((rows, columns), f32)),
        in_specs=[anywhere] * 3,
        out_specs=(anywhere, anywhere),
        scratch_shapes=[
            pltpu.VMEM((chunks, rows, CHUNK), f32),
            pltpu.VMEM((panels, S, h, nb), f32),
            pltpu.VMEM((panels, rows, nb), bf16),
            pltpu.VMEM((panels, rows, nb), bf16),
            pltpu.VMEM((panels, chunks, nb, CHUNK), f32),
            pltpu.VMEM((panels, chunks, nb, CHUNK), bf16),
            pltpu.VMEM((panels, chunks, nb, CHUNK), bf16),
            pltpu.VMEM((nb, nb), f32),
            pltpu.VMEM((nb, nb), bf16),
            pltpu.VMEM((nb, nb), bf16),
            dma((panels, S, PARTS)),
            dma((3, panels, S, PARTS)),
            dma((panels,)),
            dma((panels, chunks, PARTS)),
            dma((2, panels, chunks, PARTS)),
            dma((chunks,)),
            dma,
            dma((chunks,)),
            dma((share // math.gcd(share, nb), chunks)),
        ],
        compiler_params=pltpu.CompilerParams(
            collective_id=0, has_side_effects=True, vmem_limit_bytes=58 * 1024 * 1024
        ),
        cost_estimate=pl.CostEstimate(
            flops=6 * rows * panels * nb * columns, bytes_accessed=8 * rows * columns, transcendentals=0
        ),
    )(right_side, lower_panels, inverse_blocks)


def solution(mesh):
    placed = (P("row", "sim"), P(None, ("row", "sim"), None), P())
    return jax.shard_map(
        functools.partial(local, mesh.shape["row"], mesh.shape["sim"]),
        mesh=mesh,
        in_specs=placed,
        out_specs=(P("row", "sim"), P("row", "sim")),
        check_vma=False,
    )
```

time: 318 us -> 141 us (0.44)
  the two profiles are of different devices: /device:TPU:3 before, /device:TPU:6 now
where the time goes in v2:
time: 141 us
  Pallas kernels  130 us (92%)
  local copies, waits for them, and re-layouts  9.9 us (7%)
    pallas_call x1, Pallas kernels, local(): pl.pallas_call(functools.partial(kernel, R, S), out_shape=(jax.ShapeDtype...  130 us
    unnamed x2, local copies, waits for them, and re-layouts  9.9 us

profile of v2, /device:TPU:6, one launch (start us, length us, event | category | flops | bytes accessed | tf_op | source)
XLA Modules:
  0.0 141.0 jit_solution(4267906943838288521)
XLA Ops:
  0.6 130.4 %shard_map.50 = (f32[384,1280]{1,0:T(8,128)}, f32[1536,1280]{1,0:T(8,128)}) custom-call(f32[1536,1280]{1,0:T(8,128)} %b_hbm.1, f32[3,192,512]{2,1,0:T(8,128)} %l_hbm.1, f32[3,512,512]{2,1,0:T(8,128)} %inv_hbm.1), custom_call_target="tpu_custom_call" | custom-call | flops 18119393280 | bytes 15728640 | tf_op jit(solution)/shard_map/pallas_call | solution.py:342
  131.1 2.9 %copy.7 = f32[384,1280]{1,0:T(8,128)} copy(f32[384,1280]{1,0:T(8,128)} %get-tuple-element.4) | data formatting | bytes 3932160
  134.0 7.0 %copy.8 = f32[1536,1280]{1,0:T(8,128)} copy(f32[1536,1280]{1,0:T(8,128)} %get-tuple-element.5) | data formatting | bytes 15728640
